TPU v7x, 32 devices: a whole 2x2x4 slice. The times are simulated.
32 devices in a mesh: rows: 8 (over z, y), feat: 4 (over x, core).
Axes of the slice: x: 2, y: 2, z: 4, core: 2. Of those that a mesh axis runs over, the one named last changes fastest.
Arguments:
- acts: bfloat16 [8192, 8192], P('rows', 'feat'), may hold values from -6 to 6
- out_grads: bfloat16 [8192, 8192], P('rows', 'feat'), may hold values from -6 to 6
- proj_in: bfloat16 [8192, 256], P('feat'), may hold values from -0.0625 to 0.0625
- proj_out: bfloat16 [8192, 256], P('feat'), may hold values from -0.0625 to 0.0625
- assignment: int32 [8192], P('rows'), may hold values from 0 to 255
- codes: int32 [1024, 65536], P('rows', 'feat'), may hold values from -128 to 127
- zero_points: int32 [65536], P('feat'), may hold values from -64 to 63
- scales: float32 [65536], P('feat'), may hold values from 2e-06 to 2e-05
Outputs:
- scores: float32 [256, 1024], P('feat', 'rows')
All inputs are finite; a program needn't handle non-finite values.
Results may differ from a plain program's by a relative error of at most 0.005.
Values may be sent and summed in bfloat16 or wider, within the bound.
A program may use at most 128 MiB of HBM per device.

v0:
```python
import jax
import jax.numpy as jnp
from jax import lax
from jax.sharding import PartitionSpec as P

RANK = 256
QUERIES = 256


def local(acts, out_grads, proj_in, proj_out, assignment, codes, zero_points, scales):
    feat_count = lax.axis_size("feat")
    local_rank = RANK // feat_count
    tokens_here = acts.shape[0]
    part_inner = jnp.dot(acts, proj_in, preferred_element_type=jnp.float32)
    part_outer = jnp.dot(out_grads, proj_out, preferred_element_type=jnp.float32)
    summed_inner = lax.psum(part_inner, "feat")
    outer_local = lax.psum_scatter(part_outer, "feat", scatter_dimension=1, tiled=True)
    inner16 = summed_inner.astype(jnp.bfloat16)
    outer16 = outer_local.astype(jnp.bfloat16)
    query_ids = lax.broadcasted_iota(jnp.int32, (1, QUERIES), 1)
    onehot = (assignment[:, None] == query_ids).astype(jnp.bfloat16)
    weighted = (onehot[:, :, None] * outer16[:, None, :]).reshape(tokens_here, QUERIES * local_rank)
    partial_grads = lax.dot_general(
        weighted, inner16, (((0,), (0,)), ((), ())), preferred_element_type=jnp.float32
    )
    partial_grads = partial_grads.reshape(QUERIES, local_rank * RANK)
    store16 = (codes - zero_points[None, :]).astype(jnp.bfloat16)
    share = lax.psum_scatter(partial_grads, "rows", scatter_dimension=0, tiled=True)
    share16 = (share * scales[None, :]).astype(jnp.bfloat16)
    terms = lax.dot_general(
        lax.all_gather(share16, "rows", axis=0, tiled=True),
        store16,
        (((1,), (1,)), ((), ())),
        preferred_element_type=jnp.float32,
    )
    scores = lax.psum_scatter(terms, "feat", scatter_dimension=0, tiled=True)
    return scores


def solution(mesh):
    in_specs = (
        P("rows", "feat"),
        P("rows", "feat"),
        P("feat", None),
        P("feat", None),
        P("rows"),
        P("rows", "feat"),
        P("feat"),
        P("feat"),
    )
    out_specs = P("feat", "rows")
    return jax.shard_map(local, mesh=mesh, in_specs=in_specs, out_specs=out_specs, check_vma=False)
```

profile of v0, /device:TPU:0, one launch (start us, length us, event | category | flops | bytes accessed | tf_op | source)
XLA Modules:
  0.0 540.1 jit_solution(4550140905122356407)
XLA Ops:
  6.5 0.0 copy-start
  6.5 0.0 copy-start.5
  6.5 0.0 copy-start.4
  6.5 0.0 reduce-scatter.4.cloned.1.call-start
  6.5 1.2 copy-done
  7.8 4.5 fusion.5
  12.2 0.0 reduce-scatter.4.cloned.1.call-update
  12.2 0.0 reduce-scatter.6.cloned.1.call-start
  12.3 0.0 copy-done.5
  12.3 3.4 fusion.6
  15.8 0.0 copy-done.4
  15.8 0.1 fusion.2
  15.9 31.8 %all-reduce.1 = bf16[1024,256]{1,0:T(8,128)(2,1)S(1)} all-reduce(f32[1024,256]{1,0:T(8,128)S(1)} %fusion.6), channel_id=1, replica_groups=mesh['rows'=8,'feat'=4] {'feat'}, use_global_device_ids=true, to_apply=%region_1.0 | all-reduce | flops 262144 | bytes 1572864 | tf_op jit(solution)/shard_map/psum | solution.py:16
  47.7 0.0 reduce-scatter.4.cloned.1.call-done
  47.7 1.0 convert_element_type.20
  48.7 11.2 %broadcast_multiply_fusion = bf16[1024,256,64]{0,2,1:T(8,128)(2,1)} fusion(bf16[1024,64]{0,1:T(8,128)(2,1)S(1)} %convert_element_type.20, bf16[1024,256]{0,1:T(8,128)(2,1)S(1)} %fusion.2), kind=kLoop, calls=%fused_computation | loop fusion | flops 16777216 | bytes 34209792 | tf_op jit(solution)/shard_map/mul | solution.py:22
  59.9 18.3 %fusion.7 = f32[16384,256]{1,0:T(8,128)} fusion(bf16[1024,16384]{0,1:T(8,128)(2,1)} %bitcast.8, bf16[1024,256]{1,0:T(8,128)(2,1)S(1)} %all-reduce.1), kind=kOutput, calls=%fused_computation.11 | convolution fusion | flops 8589934592 | bytes 50855936 | tf_op jit(solution)/shard_map/dot_general | solution.py:23
  78.2 18.2 %reshape.32 = f32[256,16384]{1,0:T(8,128)} reshape(f32[16384,256]{1,0:T(8,128)} %fusion.7) | data formatting | bytes 33554432 | tf_op jit(solution)/shard_map/reshape | solution.py:26
  96.4 0.0 reduce-scatter.6.cloned.1.call-update
  96.4 0.0 all-gather.2.cloned.1.call-start
  96.4 283.6 %reduce-scatter.6.cloned.1.call-done = f32[32,16384]{1,0:T(8,128)} async-done(((f32[256,16384]{1,0:T(8,128)}), f32[32,16384]{1,0:T(8,128)}) %reduce-scatter.6.cloned.1.call-update) | async-done | bytes 2097168 | tf_op jit(solution)/shard_map/reduce_scatter | solution.py:28
  380.0 0.0 copy-done.3
  380.0 2.8 multiply_convert_fusion
  382.8 0.0 all-gather.2.cloned.1.call-update
  382.8 0.0 copy-start.1
  382.8 0.0 reduce-scatter.8.cloned.1.call-start
  382.9 124.0 %all-gather.2.cloned.1.call-done = bf16[256,16384]{1,0:T(8,128)(2,1)} async-done(((bf16[32,16384]{1,0:T(8,128)(2,1)}), bf16[256,16384]{1,0:T(8,128)(2,1)}) %all-gather.2.cloned.1.call-update) | async-done | bytes 8388624 | tf_op jit(solution)/shard_map/all_gather | solution.py:31
  506.9 0.0 copy-done.2
  506.9 8.7 %fusion = f32[256,128]{1,0:T(8,128)} fusion(bf16[256,16384]{1,0:T(8,128)(2,1)} %all-gather.2.cloned.1.call-done, s32[128,16384]{1,0:T(8,128)} %param.13, s32[16384]{0:T(1024)S(1)} %copy-done.2), kind=kOutput, calls=%fused_computation.2 | convolution fusion | flops 1077936128 | bytes 16973824 | tf_op jit(solution)/shard_map/dot_general | solution.py:30
  515.6 0.0 reduce-scatter.8.cloned.1.call-update
  515.7 17.9 %reduce-scatter.8.cloned.1.call-done = f32[64,128]{1,0:T(8,128)} async-done(((f32[256,128]{1,0:T(8,128)}), f32[64,128]{1,0:T(8,128)}) %reduce-scatter.8.cloned.1.call-update) | async-done | bytes 32784 | tf_op jit(solution)/shard_map/reduce_scatter | solution.py:36
  533.6 0.0 copy-done.1
  (2 shorter events, 0.0 us)
Async XLA Ops:
  6.5 1.2 copy-start
  6.5 5.8 %copy-start.5 = (bf16[2048,256]{1,0:T(8,128)(2,1)S(1)}, bf16[2048,256]{1,0:T(8,128)(2,1)}, u32[]{:S(2)}) copy-start(bf16[2048,256]{1,0:T(8,128)(2,1)} %param.10) | copy-start | bytes 3145732
  6.5 9.2 %copy-start.4 = (s32[1024]{0:T(1024)S(1)}, s32[1024]{0:T(1024)}, u32[]{:S(2)}) copy-start(s32[1024]{0:T(1024)} %param.12) | copy-start | bytes 12292
  6.5 41.1 %reduce-scatter.4.cloned.1.call-start = ((), (), s32[]{:S(2)}) async-start(), calls=%async_computation.3 | async-start | bytes 1310720 | tf_op jit(solution)/shard_map/reduce_scatter | solution.py:17
  12.2 367.8 %reduce-scatter.6.cloned.1.call-start = ((), (), s32[]{:S(2)}) async-start(), calls=%async_computation.4 | async-start | bytes 18874368 | tf_op jit(solution)/shard_map/reduce_scatter | solution.py:28
  96.4 283.6 %copy-start.3 = (f32[16384]{0:T(1024)S(1)}, f32[16384]{0:T(1024)}, u32[]{:S(2)}) copy-start(f32[16384]{0:T(1024)} %param.15) | copy-start | bytes 196612
  96.4 410.5 %copy-start.2 = (s32[16384]{0:T(1024)S(1)}, s32[16384]{0:T(1024)}, u32[]{:S(2)}) copy-start(s32[16384]{0:T(1024)} %param.14) | copy-start | bytes 196612
  96.4 410.5 %all-gather.2.cloned.1.call-start = ((), (), s32[]{:S(2)}) async-start(), calls=%async_computation.5 | async-start | bytes 9437184 | tf_op jit(solution)/shard_map/all_gather | solution.py:31
  382.8 150.8 %copy-start.1 = (bf16[2048,256]{1,0:T(8,128)(2,1)S(1)}, bf16[2048,256]{1,0:T(8,128)(2,1)}, u32[]{:S(2)}) copy-start(bf16[2048,256]{1,0:T(8,128)(2,1)} %param.11) | copy-start | bytes 3145732
  382.8 150.8 %reduce-scatter.8.cloned.1.call-start = ((), (), s32[]{:S(2)}) async-start(), calls=%async_computation.6 | async-start | bytes 163840 | tf_op jit(solution)/shard_map/reduce_scatter | solution.py:36
Sparse Core Ops, SparseCore 0:
  12.4 32.7 reduce-scatter.3
  96.5 283.4 reduce-scatter.5
  382.9 123.9 all-gather.1
  515.8 17.7 reduce-scatter.7
where the time goes:
time: 541 us; the launch traced here: 540 us
  waiting for transfers between devices  426 us (79%)
  matrix products  34.9 us (6%)
  blocking collectives  31.8 us (6%)
  local copies, waits for them, and re-layouts  19.4 us (4%)
  other arithmetic  15.1 us (3%)
  between operations  13.2 us (2%)
    reduce_scatter x1, waiting for transfers between devices, local(): lax.psum_scatter(partial_grads, 'rows', scatter_dimension=0, tiled=True)  284 us
    all_gather x1, waiting for transfers between devices, local(): lax.all_gather(share16, 'rows', axis=0, tiled=True)  124 us
    psum x1, blocking collectives, local(): summed_inner = lax.psum(part_inner, 'feat')  31.8 us
    dot_general x1, matrix products, local(): lax.dot_general(weighted, inner16, (((0,), (0,)), ((), ())), preferred_el...  18.3 us
    reshape x1, local copies, waits for them, and re-layouts, local(): partial_grads = partial_grads.reshape(QUERIES, local_rank * RANK)  18.2 us
    reduce_scatter x1, waiting for transfers between devices, local(): scores = lax.psum_scatter(terms, 'feat', scatter_dimension=0, tiled=True)  17.9 us
    mul x1, other arithmetic, local(): onehot[:, :, None] * outer16[:, None, :]  11.2 us
  transfers between devices with their start and end apart: 4, of which 3 were waited for; matrix products, arithmetic and copies ran while one was open for 1% of the time, Pallas kernels for 0%

commit v1 on v0

v1 whole, which is shorter than its diff:
```python
import functools
import jax
import jax.numpy as jnp
from jax import lax
from jax.experimental import pallas as pl
from jax.experimental.pallas import tpu as pltpu
from jax.sharding import PartitionSpec as P

QUERIES = 256
GROUP = 16
WINDOW = 96
ALIGN = 16
LANES = 128
MESH = pl.DeviceIdType.MESH


def exchange_kernel(nr, nf, inner_ref, outer_ref, in_all, out_all, rin, rout,
                    rs_send, rs_recv, ring_send, ring_recv, f_send, f_recv, g_send, g_recv):
    row = lax.axis_index("rows")
    me = lax.axis_index("feat")
    tq = rin.shape[1]
    odd = lax.rem(row, 2)
    pos = (1 - odd) * (row // 2) + odd * (nr - 1 - row // 2)

    def row_at(p):
        p = lax.rem(p + 2 * nr, nr)
        back = p // (nr // 2)
        return (1 - back) * (2 * p) + back * (2 * (nr - 1 - p) + 1)

    right, left = row_at(pos + 1), row_at(pos - 1)
    core = me + 1 - 2 * lax.rem(me, 2)
    half = nf // 2

    barrier = pltpu.get_barrier_semaphore()
    for d in range(1, nf):
        pl.semaphore_signal(barrier, inc=1, device_id=(row, lax.rem(me + d, nf)), device_id_type=MESH)
    for r in (right, left):
        pl.semaphore_signal(barrier, inc=1, device_id=(r, me), device_id_type=MESH)
    pl.semaphore_wait(barrier, nf + 1)

    def remote(src, dst, ssem, rsem, dev):
        return pltpu.make_async_remote_copy(
            src_ref=src, dst_ref=dst, send_sem=ssem, recv_sem=rsem, device_id=dev, device_id_type=MESH)

    sends = []
    firsts = []
    for d in range(1, nf):
        to = lax.rem(me + d, nf)
        a = remote(inner_ref.at[to], rin.at[d - 1], rs_send.at[0, d - 1], rs_recv.at[0, d - 1], (row, to))
        b = remote(outer_ref.at[to], rout.at[d - 1], rs_send.at[1, d - 1], rs_recv.at[1, d - 1], (row, to))
        a.start()
        b.start()
        firsts.append((a, b))
        sends += [a, b]
    si = inner_ref[me].astype(jnp.float32)
    for a, b in firsts:
        a.wait_recv()
    for d in range(1, nf):
        si += rin[d - 1].astype(jnp.float32)
    mine = pl.ds(pl.multiple_of(me * tq, tq), tq)
    in_all[row, mine, :] = si.astype(jnp.bfloat16)
    for a, b in firsts:
        b.wait_recv()
    so = outer_ref[me].astype(jnp.float32)
    for d in range(1, nf):
        so += rout[d - 1].astype(jnp.float32)
    out_all[row] = so.astype(jnp.bfloat16)

    steps_r = nr // 2
    steps_l = nr - 1 - steps_r

    def chunk_row(e):
        return row_at(pos - e) if e <= steps_r else row_at(pos + e - steps_r)

    def ring_copies(e, to, sem):
        r = chunk_row(e)
        return (remote(in_all.at[r, mine], in_all.at[r, mine], ring_send.at[0, sem], ring_recv.at[0, sem], (to, me)),
                remote(out_all.at[r], out_all.at[r], ring_send.at[1, sem], ring_recv.at[1, sem], (to, me)))

    def launch(e, to, sem):
        pair = ring_copies(e, to, sem)
        for c in pair:
            c.start()
            sends.append(c)
        return pair

    tails = []
    feats = {}

    def spread(e):
        r = chunk_row(e)
        block = in_all.at[r, mine]
        got = []
        for d in range(1, half):
            c = remote(block, block, f_send.at[e, d], f_recv.at[e, d], (row, lax.rem(me + 2 * d, nf)))
            c.start()
            sends.append(c)
            got.append(c)
        c = remote(block, block, f_send.at[e, 0], f_recv.at[e, 0], (row, core))
        c.start()
        sends.append(c)
        tails.append(c)
        feats[e] = got

    def pass_on(e):
        r = chunk_row(e)
        for d in range(1, half):
            feats[e][d - 1].wait_recv()
            src = lax.rem(me + nf - 2 * d, nf)
            block = in_all.at[r, pl.ds(pl.multiple_of(src * tq, tq), tq)]
            c = remote(block, block, g_send.at[e, d], g_recv.at[e, d], (row, core))
            c.start()
            sends.append(c)
            tails.append(c)

    cr = launch(0, right, 0)
    cl = launch(0, left, steps_r) if steps_l else None
    spread(0)
    late = [0]
    for s in range(steps_r):
        e = 1 + s
        fresh = [e]
        nxt = None
        cr[0].wait_recv()
        cr[1].wait_recv()
        if s + 1 < steps_r:
            nxt = launch(e, right, s + 1)
        spread(e)
        cr = nxt
        if s < steps_l:
            e = 1 + steps_r + s
            cl[0].wait_recv()
            cl[1].wait_recv()
            nxt = None
            if s + 1 < steps_l:
                nxt = launch(e, left, steps_r + s + 1)
            spread(e)
            cl = nxt
            fresh.append(e)
        for e in late:
            pass_on(e)
        late = fresh
    for e in late:
        pass_on(e)
    for c in tails:
        c.wait_recv()
    for c in sends:
        c.wait_send()


def grads_kernel(starts_ref, inner_ref, outer_ref, scales_ref, out_ref, in_w, out_w, acc):
    g = pl.program_id(0)
    nr, tokens, rank = inner_ref.shape
    local_rank = scales_ref.shape[0]
    begins = []
    loops = jnp.int32(1)
    for r in range(nr):
        begin = starts_ref[r, g] // ALIGN * ALIGN
        begins.append(begin)
        loops = jnp.maximum(loops, (starts_ref[r, g + 1] - begin + WINDOW - 1) // WINDOW)
    acc[...] = jnp.zeros_like(acc)
    ids_here = (g * GROUP + lax.broadcasted_iota(jnp.int32, (GROUP, 1), 0)).astype(jnp.float32)
    line = lax.broadcasted_iota(jnp.int32, (WINDOW, 1), 0)

    def one(k, carry):
        for r in range(nr):
            want = begins[r] + k * WINDOW
            at = pl.multiple_of(jnp.minimum(want, tokens - WINDOW), ALIGN)
            here = pl.ds(r * WINDOW, WINDOW)
            in_w[here, :] = inner_ref[r, pl.ds(at, WINDOW), :]
            rows = outer_ref[r, pl.ds(at, WINDOW), :].astype(jnp.float32)
            out_w[here, :] = jnp.where(line >= want - at, rows, 0.0)
        turned = out_w[...].T
        mask = turned[local_rank:local_rank + 1, :] == ids_here
        spread = jnp.where(mask[None], turned[:local_rank, None, :], 0.0).astype(jnp.bfloat16)
        spread = spread.reshape(local_rank * GROUP, in_w.shape[0])
        acc[...] += jnp.dot(spread, in_w[...], preferred_element_type=jnp.float32)
        return carry

    lax.fori_loop(0, loops, one, 0)
    grads = acc[...].reshape(local_rank, GROUP, rank)
    out_ref[...] = (grads * scales_ref[...][:, None, :]).astype(jnp.bfloat16)


def score_kernel(grads_ref, codes_ref, zero_ref, out_ref):
    @pl.when(pl.program_id(0) == 0)
    def _():
        out_ref[...] = jnp.zeros_like(out_ref)

    width = grads_ref.shape[2]
    total = out_ref[...]
    for i in range(grads_ref.shape[0]):
        cols = slice(i * width, (i + 1) * width)
        levels = (codes_ref[:, cols] - zero_ref[:, cols]).astype(jnp.float32).astype(jnp.bfloat16)
        total += lax.dot_general(grads_ref[i], levels, (((1,), (1,)), ((), ())),
                                 preferred_element_type=jnp.float32)
    out_ref[...] = total


def local(nr, nf, acts, out_grads, proj_in, proj_out, assignment, codes, zero_points, scales):
    tokens = acts.shape[0]
    rank = proj_in.shape[1]
    local_rank = rank // nf
    bf = jnp.bfloat16
    part_inner = jnp.dot(acts, proj_in, preferred_element_type=jnp.float32).astype(bf)
    part_outer = jnp.dot(out_grads, proj_out, preferred_element_type=jnp.float32).astype(bf)

    order = lax.iota(jnp.int32, tokens)
    key = assignment * tokens + order
    place = jnp.sum((key[:, None] < key[None, :]).astype(jnp.int32), axis=0)
    sorter = (place[None, :] == order[:, None]).astype(bf)
    both = jnp.dot(sorter, jnp.concatenate([part_inner, part_outer], 1), preferred_element_type=jnp.float32)
    inner = both[:, :rank].astype(bf).reshape(nf, tokens // nf, rank)
    ids = jnp.sum(jnp.where(place[None, :] == order[:, None], assignment[None, :], 0), axis=1)
    ids = jnp.where(lax.axis_index("feat") == 0, ids, 0).astype(bf)
    outer = both[:, rank:].astype(bf).reshape(tokens, nf, local_rank).transpose(1, 0, 2)
    wide = -(-(local_rank + 1) // LANES) * LANES
    outer = jnp.concatenate([
        outer,
        jnp.broadcast_to(ids[None, :, None], (nf, tokens, 1)),
        jnp.zeros((nf, tokens, wide - local_rank - 1), bf)], 2)
    edges = lax.iota(jnp.int32, QUERIES // GROUP + 1) * GROUP
    starts = jnp.sum((assignment[None, :] < edges[:, None]).astype(jnp.int32), axis=1)
    starts = lax.all_gather(starts, "rows")

    vmem = pl.BlockSpec(memory_space=pltpu.VMEM)
    dma = pltpu.SemaphoreType.DMA
    in_all, out_all = pl.pallas_call(
        functools.partial(exchange_kernel, nr, nf),
        out_shape=(jax.ShapeDtypeStruct((nr, tokens, rank), bf), jax.ShapeDtypeStruct((nr, tokens, wide), bf)),
        in_specs=[vmem, vmem],
        out_specs=(vmem, vmem),
        scratch_shapes=[
            pltpu.VMEM((nf - 1, tokens // nf, rank), bf),
            pltpu.VMEM((nf - 1, tokens, wide), bf),
            dma((2, nf - 1)), dma((2, nf - 1)),
            dma((2, nr)), dma((2, nr)),
            dma((nr, nf // 2)), dma((nr, nf // 2)),
            dma((nr, nf // 2)), dma((nr, nf // 2)),
        ],
        compiler_params=pltpu.CompilerParams(
            collective_id=0, has_side_effects=True, vmem_limit_bytes=48 * 2 ** 20),
    )(inner, outer)

    grads = pl.pallas_call(
        grads_kernel,
        out_shape=jax.ShapeDtypeStruct((local_rank, QUERIES, rank), bf),
        grid=(QUERIES // GROUP,),
        in_specs=[pl.BlockSpec(memory_space=pltpu.SMEM), vmem, vmem, vmem],
        out_specs=pl.BlockSpec((local_rank, GROUP, rank), lambda g: (0, g, 0)),
        scratch_shapes=[
            pltpu.VMEM((nr * WINDOW, rank), bf),
            pltpu.VMEM((nr * WINDOW, wide), jnp.float32),
            pltpu.VMEM((local_rank * GROUP, rank), jnp.float32),
        ],
        compiler_params=pltpu.CompilerParams(vmem_limit_bytes=56 * 2 ** 20),
    )(starts, in_all, out_all, scales.reshape(local_rank, rank))

    stored, features = codes.shape
    step = min(8, local_rank)
    terms = pl.pallas_call(
        score_kernel,
        out_shape=jax.ShapeDtypeStruct((QUERIES, stored), jnp.float32),
        grid=(local_rank // step,),
        in_specs=[
            pl.BlockSpec((step, QUERIES, rank), lambda i: (i, 0, 0)),
            pl.BlockSpec((stored, step * rank), lambda i: (0, i)),
            pl.BlockSpec((1, step * rank), lambda i: (0, i)),
        ],
        out_specs=pl.BlockSpec((QUERIES, stored), lambda i: (0, 0)),
        compiler_params=pltpu.CompilerParams(vmem_limit_bytes=32 * 2 ** 20),
    )(grads, codes, zero_points.reshape(1, features))
    return lax.psum_scatter(terms, "feat", scatter_dimension=0, tiled=True)


def solution(mesh):
    in_specs = (
        P("rows", "feat"),
        P("rows", "feat"),
        P("feat", None),
        P("feat", None),
        P("rows"),
        P("rows", "feat"),
        P("feat"),
        P("feat"),
    )
    out_specs = P("feat", "rows")
    body = functools.partial(local, mesh.shape["rows"], mesh.shape["feat"])
    return jax.shard_map(body, mesh=mesh, in_specs=in_specs, out_specs=out_specs, check_vma=False)
```

time: 541 us -> 154 us (0.28)
  waiting for transfers between devices: 426 us -> 18.3 us
  Pallas kernels: 0 us -> 85.1 us
  matrix products: 34.9 us -> 6.2 us
  blocking collectives: 31.8 us -> 13.1 us
  other arithmetic: 15.1 us -> 3.97 us
  local copies, waits for them, and re-layouts: 19.4 us -> 12.9 us
    reduce_scatter x3 -> x1, waiting for transfers between devices: 302 us -> 18.3 us  [local(): return lax.psum_scatter(terms, 'feat', scatter_dimension=0, tiled=True)]
    all_gather x1 -> x0, waiting for transfers between devices: 124 us -> none  [local(): lax.all_gather(share16, 'rows', axis=0, tiled=True)]
    pallas_call x0 -> x3, Pallas kernels: none -> 85.1 us  [the longest x1 62.2 us: local(): pl.pallas_call(functools.partial(exchange_kernel, nr, nf), out_shape=(jax...]
    psum x1 -> x0, blocking collectives: 31.8 us -> none  [local(): summed_inner = lax.psum(part_inner, 'feat')]
    dot_general x4 -> x3, matrix products: 34.9 us -> 6.2 us  [the longest x1 3.63 us: local(): jnp.dot(acts, proj_in, preferred_element_type=jnp.float32).astype(bf)]
    reshape x1 -> x2, local copies, waits for them, and re-layouts: 18.2 us -> 1.99 us  [the longest x1 1.48 us: local(): scales.reshape(local_rank, rank)]
    unnamed x0 -> x1, blocking collectives: none -> 13.1 us
    mul x1, other arithmetic: 11.2 us -> 0.01 us  [local(): edges = lax.iota(jnp.int32, QUERIES // GROUP + 1) * GROUP]
  transfers between devices with their start and end apart: 4 -> 1, of which waited for: 3 -> 1; matrix products, arithmetic and copies ran while one was open for 1% -> 0% of each run, Pallas kernels for 0% -> 0%
where the time goes in v1:
time: 154 us
  Pallas kernels  85.1 us (55%)
  waiting for transfers between devices  18.3 us (12%)
  between operations  14.2 us (9%)
  blocking collectives  13.1 us (9%)
  local copies, waits for them, and re-layouts  12.9 us (8%)
  matrix products  6.2 us (4%)
  other arithmetic  3.97 us (3%)
    pallas_call x1, Pallas kernels, local(): pl.pallas_call(functools.partial(exchange_kernel, nr, nf), out_shape=(jax...  62.2 us
    reduce_scatter x1, waiting for transfers between devices, local(): return lax.psum_scatter(terms, 'feat', scatter_dimension=0, tiled=True)  18.3 us
    pallas_call x1, Pallas kernels, local(): pl.pallas_call(grads_kernel, out_shape=jax.ShapeDtypeStruct((local_rank,...  18.1 us
    unnamed x1, blocking collectives  13.1 us
    unnamed x17, local copies, waits for them, and re-layouts  9.72 us
    pallas_call x1, Pallas kernels, local(): pl.pallas_call(score_kernel, out_shape=jax.ShapeDtypeStruct((QUERIES, sto...  4.85 us
    dot_general x1, matrix products, local(): jnp.dot(acts, proj_in, preferred_element_type=jnp.float32).astype(bf)  3.63 us
  transfers between devices with their start and end apart: 1, of which 1 were waited for; matrix products, arithmetic and copies ran while one was open for 0% of the time, Pallas kernels for 0%

profile of v1, /device:TPU:0, one launch (start us, length us, event | category | flops | bytes accessed | tf_op | source)
XLA Modules:
  0.0 153.7 jit_solution(7363413116750358490)
XLA Ops:
  6.5 0.0 copy-start
  6.5 0.0 reduce-scatter.2.cloned.1.call-start
  6.5 0.8 iota_add_fusion
  7.3 0.9 convert_reduce_fusion.1
  8.2 1.2 dynamic-slice
  10.1 0.2 dynamic-update-slice
  10.3 13.1 %all-reduce = s32[136]{0:T(256)S(1)} all-reduce(s32[136]{0:T(256)S(1)} %dynamic-update-slice), channel_id=2, replica_groups=mesh['rows'=8,'feat'=4] {'rows'}, use_global_device_ids=true, to_apply=%add | all-reduce | flops 136 | bytes 1088
  23.4 0.7 reshape.30.starts_ref
  24.1 0.5 convert_reduce_fusion
  24.6 1.2 select_reduce_fusion
  25.8 1.5 reshape.28.scales_ref
  27.2 0.0 copy-done
  27.2 3.6 %convolution_convert_fusion.1 = bf16[1024,256]{0,1:T(8,128)(2,1)S(1)} fusion(bf16[1024,2048]{1,0:T(8,128)(2,1)} %param.8, bf16[2048,256]{1,0:T(8,128)(2,1)S(1)} %copy-done), kind=kOutput, calls=%fused_computation.7 | convolution fusion | flops 1074003968 | bytes 5767168 | tf_op jit(solution)/shard_map/dot_general | solution.py:205
  30.9 0.0 copy-done.5
  30.9 0.1 copy-done.6
  31.0 1.3 convolution_convert_fusion
  32.3 1.3 fusion.2
  33.6 0.1 fusion.7
  33.6 0.2 copy.11
  33.9 0.5 copy.12
  34.4 0.1 pad.2.clone
  34.5 0.2 broadcast_in_dim.23
  34.7 0.6 maximum_maximum_fusion.outer_ref
  35.3 62.2 %shard_map.82 = (bf16[8,1024,256]{2,1,0:T(8,128)(2,1)}, bf16[8,1024,128]{2,1,0:T(8,128)(2,1)S(1)}) custom-call(bf16[4,256,256]{2,1,0:T(8,128)(2,1)S(1)} %bitcast.9, bf16[4,1024,128]{2,1,0:T(8,128)(2,1)S(1)} %maximum_maximum_fusion.outer_ref), custom_call_target="tpu_custom_call" | custom-call | tf_op jit(solution)/shard_map/pallas_call | solution.py:228
  97.6 1.4 copy-done.3
  98.9 18.1 %shard_map.83.grads_ref = bf16[64,256,256]{2,1,0:T(8,128)(2,1)} custom-call(s32[8,17]{1,0:T(8,128)} %reshape.30.starts_ref, bf16[8,1024,256]{2,1,0:T(8,128)(2,1)} %get-tuple-element.7.inner_ref, bf16[8,1024,128]{2,1,0:T(8,128)(2,1)} %copy-done.3, f32[64,256]{1,0:T(8,128)} %reshape.28.scales_ref), custom_call_target="tpu_custom_call" | custom-call | tf_op jit(solution)/shard_map/pallas_call | solution.py:245
  117.0 0.0 copy-done.4
  117.0 3.4 %copy-done.1 = bf16[64,256,256]{2,1,0:T(8,128)(2,1)S(1)} copy-done((bf16[64,256,256]{2,1,0:T(8,128)(2,1)S(1)}, bf16[64,256,256]{2,1,0:T(8,128)(2,1)}, u32[]{:S(2)}) %copy-start.1) | copy-done | bytes 8388632
  120.3 3.4 %copy-done.2 = s32[128,16384]{1,0:T(8,128)S(1)} copy-done((s32[128,16384]{1,0:T(8,128)S(1)}, s32[128,16384]{1,0:T(8,128)}, u32[]{:S(2)}) %copy-start.2) | copy-done | bytes 8388632
  123.7 4.9 %shard_map.84 = f32[256,128]{1,0:T(8,128)} custom-call(bf16[64,256,256]{2,1,0:T(8,128)(2,1)S(1)} %copy-done.1, s32[128,16384]{1,0:T(8,128)S(1)} %copy-done.2, s32[1,16384]{1,0:T(1,128)S(1)} %bitcast.10), custom_call_target="tpu_custom_call" | custom-call | tf_op jit(solution)/shard_map/pallas_call | solution.py:261
  128.6 0.0 reduce-scatter.2.cloned.1.call-update
  128.6 18.3 %reduce-scatter.2.cloned.1.call-done = f32[64,128]{1,0:T(8,128)} async-done(((f32[256,128]{1,0:T(8,128)}), f32[64,128]{1,0:T(8,128)}) %reduce-scatter.2.cloned.1.call-update) | async-done | bytes 32784 | tf_op jit(solution)/shard_map/reduce_scatter | solution.py:273
  (10 shorter events, 0.0 us)
Async XLA Ops:
  6.5 20.7 %copy-start = (bf16[2048,256]{1,0:T(8,128)(2,1)S(1)}, bf16[2048,256]{1,0:T(8,128)(2,1)}, u32[]{:S(2)}) copy-start(bf16[2048,256]{1,0:T(8,128)(2,1)} %param.10) | copy-start | bytes 3145732
  6.5 140.3 %reduce-scatter.2.cloned.1.call-start = ((), (), s32[]{:S(2)}) async-start(), calls=%async_computation.1 | async-start | bytes 163840 | tf_op jit(solution)/shard_map/reduce_scatter | solution.py:273
  27.2 3.6 %copy-start.5 = (bf16[1024,2048]{1,0:T(8,128)(2,1)S(1)}, bf16[1024,2048]{1,0:T(8,128)(2,1)}, u32[]{:S(2)}) copy-start(bf16[1024,2048]{1,0:T(8,128)(2,1)} %param.9) | copy-start | bytes 12582916
  27.2 3.7 %copy-start.6 = (bf16[2048,256]{1,0:T(8,128)(2,1)S(1)}, bf16[2048,256]{1,0:T(8,128)(2,1)}, u32[]{:S(2)}) copy-start(bf16[2048,256]{1,0:T(8,128)(2,1)} %param.11) | copy-start | bytes 3145732
  97.5 1.4 copy-start.3
  98.9 18.1 %copy-start.4 = (s32[16384]{0:T(1024)S(1)}, s32[16384]{0:T(1024)}, u32[]{:S(2)}) copy-start(s32[16384]{0:T(1024)} %param.14) | copy-start | bytes 196612
  117.0 3.4 %copy-start.1 = (bf16[64,256,256]{2,1,0:T(8,128)(2,1)S(1)}, bf16[64,256,256]{2,1,0:T(8,128)(2,1)}, u32[]{:S(2)}) copy-start(bf16[64,256,256]{2,1,0:T(8,128)(2,1)} %shard_map.83.grads_ref) | copy-start | bytes 25165828
  120.3 3.4 %copy-start.2 = (s32[128,16384]{1,0:T(8,128)S(1)}, s32[128,16384]{1,0:T(8,128)}, u32[]{:S(2)}) copy-start(s32[128,16384]{1,0:T(8,128)} %codes_ref.1) | copy-start | bytes 25165828
Sparse Core Ops, SparseCore 0:
  128.7 18.0 reduce-scatter.1

commit v2 on v1

--- a/solution.py
+++ b/solution.py
@@ -14,11 +14,12 @@
 MESH = pl.DeviceIdType.MESH
 
 
-def exchange_kernel(nr, nf, inner_ref, outer_ref, in_all, out_all, rin, rout,
-                    rs_send, rs_recv, ring_send, ring_recv, f_send, f_recv, g_send, g_recv):
+def exchange_kernel(nr, nf, local_rank, inner_ref, outer_ref, ids_ref, in_all, out_all,
+                    rin, rout, far_in, far_out, to_in, to_out, rs_send, rs_recv, far_send, far_recv,
+                    ring_send, ring_recv, f_send, f_recv, g_send, g_recv):
     row = lax.axis_index("rows")
     me = lax.axis_index("feat")
-    tq = rin.shape[1]
+    tq, wide = rin.shape[1], rout.shape[2]
     odd = lax.rem(row, 2)
     pos = (1 - odd) * (row // 2) + odd * (nr - 1 - row // 2)
 
@@ -32,39 +33,65 @@
     half = nf // 2
 
     barrier = pltpu.get_barrier_semaphore()
-    for d in range(1, nf):
-        pl.semaphore_signal(barrier, inc=1, device_id=(row, lax.rem(me + d, nf)), device_id_type=MESH)
+    for d in range(1, half):
+        pl.semaphore_signal(barrier, inc=1, device_id=(row, lax.rem(me + 2 * d, nf)), device_id_type=MESH)
+    pl.semaphore_signal(barrier, inc=1, device_id=(row, core), device_id_type=MESH)
     for r in (right, left):
         pl.semaphore_signal(barrier, inc=1, device_id=(r, me), device_id_type=MESH)
-    pl.semaphore_wait(barrier, nf + 1)
+    pl.semaphore_wait(barrier, half + 2)
 
     def remote(src, dst, ssem, rsem, dev):
         return pltpu.make_async_remote_copy(
             src_ref=src, dst_ref=dst, send_sem=ssem, recv_sem=rsem, device_id=dev, device_id_type=MESH)
 
     sends = []
-    firsts = []
-    for d in range(1, nf):
-        to = lax.rem(me + d, nf)
-        a = remote(inner_ref.at[to], rin.at[d - 1], rs_send.at[0, d - 1], rs_recv.at[0, d - 1], (row, to))
-        b = remote(outer_ref.at[to], rout.at[d - 1], rs_send.at[1, d - 1], rs_recv.at[1, d - 1], (row, to))
-        a.start()
-        b.start()
-        firsts.append((a, b))
-        sends += [a, b]
-    si = inner_ref[me].astype(jnp.float32)
-    for a, b in firsts:
-        a.wait_recv()
-    for d in range(1, nf):
-        si += rin[d - 1].astype(jnp.float32)
+
+    def begin(*args):
+        c = remote(*args)
+        c.start()
+        sends.append(c)
+        return c
+
+    lane = lax.broadcasted_iota(jnp.int32, (1, wide), 1)
+
+    def unpack(packed):
+        both = packed.astype(jnp.float32)
+        return both + pltpu.roll(both, wide - local_rank, 1)
+
+    def pack(total):
+        high = total.astype(jnp.bfloat16).astype(jnp.float32)
+        low = pltpu.roll(total - high, local_rank, 1)
+        return jnp.where(lane < local_rank, high, low).astype(jnp.bfloat16)
+
+    near = {}
+    for d in list(range(1, half)) + [0]:
+        to = lax.rem(core + 2 * d, nf)
+        near[d] = (begin(inner_ref.at[to], rin.at[d], rs_send.at[0, d], rs_recv.at[0, d], (row, core)),
+                   begin(outer_ref.at[to], rout.at[d], rs_send.at[1, d], rs_recv.at[1, d], (row, core)))
+    far = {}
+    for d in range(1, half):
+        to = lax.rem(me + 2 * d, nf)
+        near[d][0].wait_recv()
+        to_in[d - 1] = inner_ref[to] + rin[d]
+        one = begin(to_in.at[d - 1], far_in.at[d - 1], far_send.at[0, d], far_recv.at[0, d], (row, to))
+        near[d][1].wait_recv()
+        to_out[d - 1] = pack(unpack(outer_ref[to]) + unpack(rout[d]))
+        two = begin(to_out.at[d - 1], far_out.at[d - 1], far_send.at[1, d], far_recv.at[1, d], (row, to))
+        far[d] = (one, two)
     mine = pl.ds(pl.multiple_of(me * tq, tq), tq)
-    in_all[row, mine, :] = si.astype(jnp.bfloat16)
-    for a, b in firsts:
-        b.wait_recv()
-    so = outer_ref[me].astype(jnp.float32)
-    for d in range(1, nf):
-        so += rout[d - 1].astype(jnp.float32)
-    out_all[row] = so.astype(jnp.bfloat16)
+    near[0][0].wait_recv()
+    total = inner_ref[me] + rin[0]
+    for d in range(1, half):
+        far[d][0].wait_recv()
+        total += far_in[d - 1]
+    in_all[row, mine, :] = total.astype(jnp.bfloat16)
+    near[0][1].wait_recv()
+    total = unpack(outer_ref[me]) + unpack(rout[0])
+    for d in range(1, half):
+        far[d][1].wait_recv()
+        total += unpack(far_out[d - 1])
+    total = jnp.where(lane < local_rank, total, jnp.where(lane == local_rank, ids_ref[...], 0.0))
+    out_all[row] = total.astype(jnp.bfloat16)
 
     steps_r = nr // 2
     steps_l = nr - 1 - steps_r
@@ -72,13 +99,13 @@
     def chunk_row(e):
         return row_at(pos - e) if e <= steps_r else row_at(pos + e - steps_r)
 
-    def ring_copies(e, to, sem):
+    def ring_copy(e, to, sem, w):
         r = chunk_row(e)
-        return (remote(in_all.at[r, mine], in_all.at[r, mine], ring_send.at[0, sem], ring_recv.at[0, sem], (to, me)),
-                remote(out_all.at[r], out_all.at[r], ring_send.at[1, sem], ring_recv.at[1, sem], (to, me)))
-
-    def launch(e, to, sem):
-        pair = ring_copies(e, to, sem)
+        block = out_all.at[r] if w else in_all.at[r, mine]
+        return remote(block, block, ring_send.at[w, sem], ring_recv.at[w, sem], (to, me))
+
+    def launch(e, to, sem, which=(0, 1)):
+        pair = [ring_copy(e, to, sem, w) for w in which]
         for c in pair:
             c.start()
             sends.append(c)
@@ -114,28 +141,23 @@
             tails.append(c)
 
     cr = launch(0, right, 0)
-    cl = launch(0, left, steps_r) if steps_l else None
+    cl = launch(0, left, steps_r)
     spread(0)
     late = [0]
     for s in range(steps_r):
         e = 1 + s
         fresh = [e]
-        nxt = None
-        cr[0].wait_recv()
-        cr[1].wait_recv()
+        for c in cr:
+            c.wait_recv()
         if s + 1 < steps_r:
-            nxt = launch(e, right, s + 1)
+            cr = launch(e, right, s + 1, (0, 1) if s + 2 < steps_r else (0,))
         spread(e)
-        cr = nxt
+        for c in cl:
+            c.wait_recv()
         if s < steps_l:
             e = 1 + steps_r + s
-            cl[0].wait_recv()
-            cl[1].wait_recv()
-            nxt = None
-            if s + 1 < steps_l:
-                nxt = launch(e, left, steps_r + s + 1)
+            cl = launch(e, left, steps_r + s + 1, (0, 1) if s + 1 < steps_l else (1,))
             spread(e)
-            cl = nxt
             fresh.append(e)
         for e in late:
             pass_on(e)
@@ -145,6 +167,31 @@
     for c in tails:
         c.wait_recv()
     for c in sends:
+        c.wait_send()
+
+
+def total_kernel(nf, terms_ref, out_ref, got, send, recv):
+    row = lax.axis_index("rows")
+    me = lax.axis_index("feat")
+    count = out_ref.shape[0]
+    barrier = pltpu.get_barrier_semaphore()
+    for d in range(1, nf):
+        pl.semaphore_signal(barrier, inc=1, device_id=(row, lax.rem(me + d, nf)), device_id_type=MESH)
+    pl.semaphore_wait(barrier, nf - 1)
+    copies = []
+    for d in range(1, nf):
+        to = lax.rem(me + d, nf)
+        c = pltpu.make_async_remote_copy(
+            src_ref=terms_ref.at[pl.ds(pl.multiple_of(to * count, count), count)], dst_ref=got.at[d - 1],
+            send_sem=send.at[d - 1], recv_sem=recv.at[d - 1], device_id=(row, to), device_id_type=MESH)
+        c.start()
+        copies.append(c)
+    total = terms_ref[pl.ds(pl.multiple_of(me * count, count), count), :]
+    for d in range(1, nf):
+        copies[d - 1].wait_recv()
+        total += got[d - 1]
+    out_ref[...] = total
+    for c in copies:
         c.wait_send()
 
 
@@ -202,45 +249,52 @@
     rank = proj_in.shape[1]
     local_rank = rank // nf
     bf = jnp.bfloat16
-    part_inner = jnp.dot(acts, proj_in, preferred_element_type=jnp.float32).astype(bf)
-    part_outer = jnp.dot(out_grads, proj_out, preferred_element_type=jnp.float32).astype(bf)
+    parts = [jnp.dot(acts, proj_in, preferred_element_type=jnp.float32),
+             jnp.dot(out_grads, proj_out, preferred_element_type=jnp.float32)]
 
     order = lax.iota(jnp.int32, tokens)
     key = assignment * tokens + order
     place = jnp.sum((key[:, None] < key[None, :]).astype(jnp.int32), axis=0)
-    sorter = (place[None, :] == order[:, None]).astype(bf)
-    both = jnp.dot(sorter, jnp.concatenate([part_inner, part_outer], 1), preferred_element_type=jnp.float32)
-    inner = both[:, :rank].astype(bf).reshape(nf, tokens // nf, rank)
-    ids = jnp.sum(jnp.where(place[None, :] == order[:, None], assignment[None, :], 0), axis=1)
-    ids = jnp.where(lax.axis_index("feat") == 0, ids, 0).astype(bf)
-    outer = both[:, rank:].astype(bf).reshape(tokens, nf, local_rank).transpose(1, 0, 2)
-    wide = -(-(local_rank + 1) // LANES) * LANES
-    outer = jnp.concatenate([
-        outer,
-        jnp.broadcast_to(ids[None, :, None], (nf, tokens, 1)),
-        jnp.zeros((nf, tokens, wide - local_rank - 1), bf)], 2)
-    edges = lax.iota(jnp.int32, QUERIES // GROUP + 1) * GROUP
-    starts = jnp.sum((assignment[None, :] < edges[:, None]).astype(jnp.int32), axis=1)
-    starts = lax.all_gather(starts, "rows")
+    hits = place[None, :] == order[:, None]
+    sorter = hits.astype(bf)
+    highs = [p.astype(bf) for p in parts]
+    lows = [(p - h.astype(jnp.float32)).astype(bf) for p, h in zip(parts, highs)]
+    both = jnp.dot(sorter, jnp.concatenate(highs + lows, 1), preferred_element_type=jnp.float32)
+    inner = (both[:, :rank] + both[:, 2 * rank:3 * rank]).reshape(nf, tokens // nf, rank)
+    ids = jnp.sum(jnp.where(hits, assignment[None, :], 0), axis=1).astype(jnp.float32)[:, None]
+    wide = -(-2 * local_rank // LANES) * LANES
+    high, low = both[:, rank:2 * rank].astype(bf), both[:, 3 * rank:].astype(bf)
+    fill = [jnp.zeros((tokens, wide - 2 * local_rank), bf)] if wide > 2 * local_rank else []
+    outer = jnp.stack([
+        jnp.concatenate([high[:, i * local_rank:(i + 1) * local_rank],
+                         low[:, i * local_rank:(i + 1) * local_rank]] + fill, 1) for i in range(nf)])
 
     vmem = pl.BlockSpec(memory_space=pltpu.VMEM)
     dma = pltpu.SemaphoreType.DMA
     in_all, out_all = pl.pallas_call(
-        functools.partial(exchange_kernel, nr, nf),
+        functools.partial(exchange_kernel, nr, nf, local_rank),
         out_shape=(jax.ShapeDtypeStruct((nr, tokens, rank), bf), jax.ShapeDtypeStruct((nr, tokens, wide), bf)),
-        in_specs=[vmem, vmem],
+        in_specs=[vmem, vmem, vmem],
         out_specs=(vmem, vmem),
         scratch_shapes=[
-            pltpu.VMEM((nf - 1, tokens // nf, rank), bf),
-            pltpu.VMEM((nf - 1, tokens, wide), bf),
-            dma((2, nf - 1)), dma((2, nf - 1)),
+            pltpu.VMEM((nf // 2, tokens // nf, rank), jnp.float32),
+            pltpu.VMEM((nf // 2, tokens, wide), bf),
+            pltpu.VMEM((nf // 2 - 1, tokens // nf, rank), jnp.float32),
+            pltpu.VMEM((nf // 2 - 1, tokens, wide), bf),
+            pltpu.VMEM((nf // 2 - 1, tokens // nf, rank), jnp.float32),
+            pltpu.VMEM((nf // 2 - 1, tokens, wide), bf),
+            dma((2, nf // 2)), dma((2, nf // 2)),
+            dma((2, nf // 2)), dma((2, nf // 2)),
             dma((2, nr)), dma((2, nr)),
             dma((nr, nf // 2)), dma((nr, nf // 2)),
             dma((nr, nf // 2)), dma((nr, nf // 2)),
         ],
         compiler_params=pltpu.CompilerParams(
             collective_id=0, has_side_effects=True, vmem_limit_bytes=48 * 2 ** 20),
-    )(inner, outer)
+    )(inner, outer, ids)
+    edges = lax.iota(jnp.int32, QUERIES // GROUP + 1) * GROUP
+    found = out_all[:, :, local_rank].astype(jnp.int32)
+    starts = jnp.sum((found[:, None, :] < edges[None, :, None]).astype(jnp.int32), axis=2)
 
     grads = pl.pallas_call(
         grads_kernel,
@@ -268,9 +322,16 @@
             pl.BlockSpec((1, step * rank), lambda i: (0, i)),
         ],
         out_specs=pl.BlockSpec((QUERIES, stored), lambda i: (0, 0)),
-        compiler_params=pltpu.CompilerParams(vmem_limit_bytes=32 * 2 ** 20),
+        compiler_params=pltpu.CompilerParams(vmem_limit_bytes=56 * 2 ** 20),
     )(grads, codes, zero_points.reshape(1, features))
-    return lax.psum_scatter(terms, "feat", scatter_dimension=0, tiled=True)
+    return pl.pallas_call(
+        functools.partial(total_kernel, nf),
+        out_shape=jax.ShapeDtypeStruct((QUERIES // nf, stored), jnp.float32),
+        in_specs=[vmem],
+        out_specs=vmem,
+        scratch_shapes=[pltpu.VMEM((nf - 1, QUERIES // nf, stored), jnp.float32), dma((nf - 1,)), dma((nf - 1,))],
+        compiler_params=pltpu.CompilerParams(collective_id=1, has_side_effects=True),
+    )(terms)
 
 
 def solution(mesh):

time: 154 us -> 123 us (0.80)
  waiting for transfers between devices: 18.3 us -> 0 us
  between operations: 14.2 us -> 0.14 us
  blocking collectives: 13.1 us -> 0 us
  Pallas kernels: 85.1 us -> 95.3 us
  other arithmetic: 3.97 us -> 6.52 us
    reduce_scatter x1 -> x0, waiting for transfers between devices: 18.3 us -> none  [local(): return lax.psum_scatter(terms, 'feat', scatter_dimension=0, tiled=True)]
    unnamed x1 -> x0, blocking collectives: 13.1 us -> none
    unnamed x17 -> x15, local copies, waits for them, and re-layouts: 9.72 us -> 3.54 us
    pallas_call x1, Pallas kernels: 4.85 us -> 9.72 us  [local(): pl.pallas_call(score_kernel, out_shape=jax.ShapeDtypeStruct((QUERIES, sto...]
    pallas_call x1 -> x2, Pallas kernels: 62.2 us -> 66.9 us  [the longest x1 61.2 us: local(): pl.pallas_call(functools.partial(exchange_kernel, nr, nf, local_rank), ou...]
    dot_general x0 -> x1, local copies, waits for them, and re-layouts: none -> 3.34 us  [local(): jnp.dot(sorter, jnp.concatenate(highs + lows, 1), preferred_element_type=...]
    add x0 -> x1, local copies, waits for them, and re-layouts: none -> 2.54 us  [local(): both[:, :rank] + both[:, 2 * rank:3 * rank]]
    convert_element_type x1 -> x2, other arithmetic: 0.01 us -> 1.75 us  [the longest x1 1.74 us: local(): found = out_all[:, :, local_rank].astype(jnp.int32)]
  transfers between devices with their start and end apart: 1 -> 0, of which waited for: 1 -> 0; matrix products, arithmetic and copies ran while one was open for 0% -> 0% of each run, Pallas kernels for 0% -> 0%
where the time goes in v2:
time: 123 us; the launch traced here: 122 us
  Pallas kernels  95.3 us (77%)
  local copies, waits for them, and re-layouts  13.1 us (11%)
  matrix products  7.32 us (6%)
  other arithmetic  6.52 us (5%)
    pallas_call x1, Pallas kernels, local(): pl.pallas_call(functools.partial(exchange_kernel, nr, nf, local_rank), ou...  61.2 us
    pallas_call x1, Pallas kernels, local(): pl.pallas_call(grads_kernel, out_shape=jax.ShapeDtypeStruct((local_rank,...  18.7 us
    pallas_call x1, Pallas kernels, local(): pl.pallas_call(score_kernel, out_shape=jax.ShapeDtypeStruct((QUERIES, sto...  9.72 us
    pallas_call x1, Pallas kernels, local(): pl.pallas_call(functools.partial(total_kernel, nf), out_shape=jax.ShapeDt...  5.68 us
    dot_general x1, matrix products, local(): jnp.dot(acts, proj_in, preferred_element_type=jnp.float32)  3.63 us
    unnamed x15, local copies, waits for them, and re-layouts  3.54 us
    dot_general x1, local copies, waits for them, and re-layouts, local(): jnp.dot(sorter, jnp.concatenate(highs + lows, 1), preferred_element_type=...  3.34 us
    add x1, local copies, waits for them, and re-layouts, local(): both[:, :rank] + both[:, 2 * rank:3 * rank]  2.54 us

profile of v2, /device:TPU:0, one launch (start us, length us, event | category | flops | bytes accessed | tf_op | source)
XLA Modules:
  0.0 122.4 jit_solution(5662272670791642357)
XLA Ops:
  0.0 0.0 copy-start
  0.0 0.8 iota_add_fusion
  0.8 0.5 convert_reduce_fusion.1
  1.3 1.2 select_reduce_fusion
  2.5 1.5 %reshape.33.scales_ref = f32[64,256]{1,0:T(8,128)} reshape(f32[16384]{0:T(1024)} %param.15) | data formatting | bytes 131072 | tf_op jit(solution)/shard_map/reshape | solution.py:311
  4.0 1.0 copy.16.ids_ref
  5.0 0.0 copy-done
  5.0 3.6 %subtract_convert_fusion.1 = (bf16[1024,256]{0,1:T(8,128)(2,1)S(1)}, bf16[1024,256]{0,1:T(8,128)(2,1)S(1)}) fusion(bf16[1024,2048]{1,0:T(8,128)(2,1)} %param.8, bf16[2048,256]{1,0:T(8,128)(2,1)S(1)} %copy-done), kind=kOutput, calls=%fused_computation.16 | convolution fusion | flops 1074790400 | bytes 6291456 | tf_op jit(solution)/shard_map/dot_general | solution.py:252
  8.6 0.0 copy-done.5
  8.7 0.1 copy-done.6
  8.7 1.3 %subtract_convert_fusion = (bf16[1024,256]{0,1:T(8,128)(2,1)S(1)}, bf16[1024,256]{0,1:T(8,128)(2,1)S(1)}) fusion(bf16[1024,2048]{1,0:T(8,128)(2,1)S(1)} %copy-done.5, bf16[2048,256]{1,0:T(8,128)(2,1)S(1)} %copy-done.6), kind=kOutput, calls=%fused_computation.15 | convolution fusion | flops 1074790400 | bytes 6291456 | tf_op jit(solution)/shard_map/dot_general | solution.py:253
  10.0 2.4 %fusion = f32[1024,1024]{0,1:T(8,128)S(1)} fusion(bf16[1024,256]{0,1:T(8,128)(2,1)S(1)} %get-tuple-element.11, bf16[1024,256]{0,1:T(8,128)(2,1)S(1)} %get-tuple-element.9, bf16[1024,256]{0,1:T(8,128)(2,1)S(1)} %get-tuple-element.12, bf16[1024,256]{0,1:T(8,128)(2,1)S(1)} %get-tuple-element.10, s32[1024]{0:T(1024)S(1)} %convert_reduce_fusion.1), kind=kOutput, calls=%fused_computation.3 | convolution fusion | flops 2156920832 | bytes 6295552 | tf_op jit(solution)/shard_map/dot_general | solution.py:262
  12.5 0.0 copy-start.4
  12.5 1.9 %copy-done.4 = f32[1024,1024]{0,1:T(8,128)} copy-done((f32[1024,1024]{0,1:T(8,128)}, f32[1024,1024]{0,1:T(8,128)S(1)}, u32[]{:S(2)}) %copy-start.4) | copy-done | bytes 4194328
  14.4 1.1 slice_add_fusion
  15.5 3.3 %copy.15 = bf16[1024,1024]{1,0:T(8,128)(2,1)S(1)} copy(f32[1024,1024]{0,1:T(8,128)} %copy-done.4) | data formatting | bytes 6291456 | tf_op jit(solution)/shard_map/dot_general | solution.py:262
  18.9 2.5 %copy.14 = f32[1024,256]{1,0:T(8,128)} copy(f32[1024,256]{0,1:T(8,128)} %slice_add_fusion) | data formatting | bytes 2097152 | tf_op jit(solution)/shard_map/add | solution.py:263
  21.4 0.5 fusion.10
  21.9 0.3 maximum_bitcast_fusion
  22.2 0.3 maximum_bitcast_fusion.2
  22.5 0.1 pad_maximum_fusion.outer_ref
  22.7 0.1 copy-done.3
  22.8 61.2 %shard_map.82 = (bf16[8,1024,256]{2,1,0:T(8,128)(2,1)}, bf16[8,1024,128]{2,1,0:T(8,128)(2,1)S(1)}) custom-call(f32[4,256,256]{2,1,0:T(8,128)S(1)} %bitcast.15, bf16[4,1024,128]{2,1,0:T(8,128)(2,1)S(1)} %pad_maximum_fusion.outer_ref, f32[1024,1]{1,0:T(8,128)S(1)} %copy-done.3), custom_call_target="tpu_custom_call" | custom-call | tf_op jit(solution)/shard_map/pallas_call | solution.py:274
  84.0 0.0 copy-start.1
  84.0 1.7 %convert_reduce_fusion = s32[8,1024]{1,0:T(8,128)S(1)} fusion(bf16[8,1024,128]{2,1,0:T(8,128)(2,1)S(1)} %get-tuple-element.7.outer_ref), kind=kLoop, calls=%fused_computation | loop fusion | flops 8192 | bytes 49152 | tf_op jit(solution)/shard_map/convert_element_type | solution.py:296
  85.7 0.5 convert_reduce_fusion.2
  86.2 0.7 copy.17.starts_ref
  86.9 0.0 copy-done.1
  86.9 18.7 %shard_map.83.grads_ref = bf16[64,256,256]{2,1,0:T(8,128)(2,1)} custom-call(s32[8,17]{1,0:T(8,128)} %copy.17.starts_ref, bf16[8,1024,256]{2,1,0:T(8,128)(2,1)} %get-tuple-element.8.inner_ref, bf16[8,1024,128]{2,1,0:T(8,128)(2,1)} %copy-done.1, f32[64,256]{1,0:T(8,128)} %reshape.33.scales_ref), custom_call_target="tpu_custom_call" | custom-call | tf_op jit(solution)/shard_map/pallas_call | solution.py:299
  105.6 9.7 %shard_map.84.terms_ref = f32[256,128]{1,0:T(8,128)} custom-call(bf16[64,256,256]{2,1,0:T(8,128)(2,1)} %shard_map.83.grads_ref, s32[128,16384]{1,0:T(8,128)} %codes_ref.1, s32[1,16384]{1,0:T(1,128)} %bitcast.16), custom_call_target="tpu_custom_call" | custom-call | tf_op jit(solution)/shard_map/pallas_call | solution.py:315
  115.3 5.7 %shard_map.85 = f32[64,128]{1,0:T(8,128)} custom-call(f32[256,128]{1,0:T(8,128)} %shard_map.84.terms_ref), custom_call_target="tpu_custom_call" | custom-call | tf_op jit(solution)/shard_map/pallas_call | solution.py:327
  121.0 1.4 %copy.19 = f32[64,128]{1,0:T(8,128)} copy(f32[64,128]{1,0:T(8,128)} %shard_map.85) | data formatting | bytes 65536
  (7 shorter events, 0.0 us)
Async XLA Ops:
  0.0 5.0 %copy-start = (bf16[2048,256]{1,0:T(8,128)(2,1)S(1)}, bf16[2048,256]{1,0:T(8,128)(2,1)}, u32[]{:S(2)}) copy-start(bf16[2048,256]{1,0:T(8,128)(2,1)} %param.10) | copy-start | bytes 3145732
  5.0 3.6 %copy-start.5 = (bf16[1024,2048]{1,0:T(8,128)(2,1)S(1)}, bf16[1024,2048]{1,0:T(8,128)(2,1)}, u32[]{:S(2)}) copy-start(bf16[1024,2048]{1,0:T(8,128)(2,1)} %param.9) | copy-start | bytes 12582916
  5.0 3.7 %copy-start.6 = (bf16[2048,256]{1,0:T(8,128)(2,1)S(1)}, bf16[2048,256]{1,0:T(8,128)(2,1)}, u32[]{:S(2)}) copy-start(bf16[2048,256]{1,0:T(8,128)(2,1)} %param.11) | copy-start | bytes 3145732
  12.5 1.9 %copy-start.4 = (f32[1024,1024]{0,1:T(8,128)}, f32[1024,1024]{0,1:T(8,128)S(1)}, u32[]{:S(2)}) copy-start(f32[1024,1024]{0,1:T(8,128)S(1)} %fusion) | copy-start | bytes 12582916
  21.4 1.2 %copy-start.2 = (f32[1024,256]{1,0:T(8,128)S(1)}, f32[1024,256]{1,0:T(8,128)}, u32[]{:S(2)}) copy-start(f32[1024,256]{1,0:T(8,128)} %copy.14) | copy-start | bytes 3145732
  21.4 1.4 %copy-start.3 = (f32[1024,1]{1,0:T(8,128)S(1)}, f32[1024,1]{1,0:T(8,128)}, u32[]{:S(2)}) copy-start(f32[1024,1]{1,0:T(8,128)} %copy.16.ids_ref) | copy-start | bytes 12292
  84.0 2.9 %copy-start.1 = (bf16[8,1024,128]{2,1,0:T(8,128)(2,1)}, bf16[8,1024,128]{2,1,0:T(8,128)(2,1)S(1)}, u32[]{:S(2)}) copy-start(bf16[8,1024,128]{2,1,0:T(8,128)(2,1)S(1)} %get-tuple-element.7.outer_ref) | copy-start | bytes 6291460

commit v3 on v2

--- a/solution.py
+++ b/solution.py
@@ -12,6 +12,43 @@
 ALIGN = 16
 LANES = 128
 MESH = pl.DeviceIdType.MESH
+
+
+def project_kernel(nf, row_ref, col_ref, acts_ref, grads_ref, in_ref, out_ref, inner_ref, outer_ref, ids_ref, parts):
+    i = pl.program_id(0)
+    rank = in_ref.shape[1]
+    local_rank = rank // nf
+    block, tokens = acts_ref.shape[0], parts.shape[0]
+    bf = jnp.bfloat16
+    here = pl.ds(pl.multiple_of(i * block, block), block)
+    for k, (x, w) in enumerate(((acts_ref, in_ref), (grads_ref, out_ref))):
+        part = jnp.dot(x[...], w[...], preferred_element_type=jnp.float32)
+        high = part.astype(bf)
+        parts[here, k * rank:(k + 1) * rank] = high
+        parts[here, (2 + k) * rank:(3 + k) * rank] = (part - high.astype(jnp.float32)).astype(bf)
+
+    @pl.when(i == pl.num_programs(0) - 1)
+    def _():
+        owners = row_ref[...]
+        key = owners * tokens + lax.broadcasted_iota(jnp.int32, (1, tokens), 1)
+        line = lax.broadcasted_iota(jnp.int32, (LANES, 1), 0)
+        place = jnp.zeros((1, tokens), jnp.int32)
+        for c in range(tokens // LANES):
+            other = col_ref[c * LANES:(c + 1) * LANES, :] * tokens + (line + c * LANES)
+            place += jnp.sum(jnp.where(other < key, 1, 0), axis=0, keepdims=True)
+        names = owners.astype(jnp.float32)
+        for c in range(tokens // LANES):
+            rows = slice(c * LANES, (c + 1) * LANES)
+            hits = place == line + c * LANES
+            both = jnp.dot(jnp.where(hits, 1.0, 0.0).astype(bf), parts[...], preferred_element_type=jnp.float32)
+            inner_ref[rows, :] = both[:, :rank] + both[:, 2 * rank:3 * rank]
+            ids_ref[rows, :] = jnp.sum(jnp.where(hits, names, 0.0), axis=1, keepdims=True)
+            for d in range(nf):
+                pieces = [both[:, k * rank + d * local_rank:k * rank + (d + 1) * local_rank] for k in (1, 3)]
+                rest = outer_ref.shape[2] - 2 * local_rank
+                if rest:
+                    pieces.append(jnp.zeros((LANES, rest), jnp.float32))
+                outer_ref[d, rows, :] = jnp.concatenate(pieces, 1).astype(bf)
 
 
 def exchange_kernel(nr, nf, local_rank, inner_ref, outer_ref, ids_ref, in_all, out_all,
@@ -195,8 +232,7 @@
         c.wait_send()
 
 
-def grads_kernel(starts_ref, inner_ref, outer_ref, scales_ref, out_ref, in_w, out_w, acc):
-    g = pl.program_id(0)
+def group_grads(g, starts_ref, inner_ref, outer_ref, scales_ref, held, in_w, out_w, acc):
     nr, tokens, rank = inner_ref.shape
     local_rank = scales_ref.shape[0]
     begins = []
@@ -226,22 +262,33 @@
 
     lax.fori_loop(0, loops, one, 0)
     grads = acc[...].reshape(local_rank, GROUP, rank)
-    out_ref[...] = (grads * scales_ref[...][:, None, :]).astype(jnp.bfloat16)
-
-
-def score_kernel(grads_ref, codes_ref, zero_ref, out_ref):
-    @pl.when(pl.program_id(0) == 0)
+    scaled = (grads * scales_ref[...][:, None, :]).astype(jnp.bfloat16)
+    held[:, pl.ds(pl.multiple_of(g * GROUP, GROUP), GROUP), :] = scaled
+
+
+def score_kernel(step, starts_ref, inner_ref, outer_ref, scales_ref, codes_ref, zero_ref, out_ref,
+                 in_w, out_w, acc, held):
+    g = pl.program_id(0)
+    groups = QUERIES // GROUP
+
+    @pl.when(g < groups)
+    def _():
+        group_grads(g, starts_ref, inner_ref, outer_ref, scales_ref, held, in_w, out_w, acc)
+
+    @pl.when(g == groups)
     def _():
         out_ref[...] = jnp.zeros_like(out_ref)
 
-    width = grads_ref.shape[2]
-    total = out_ref[...]
-    for i in range(grads_ref.shape[0]):
-        cols = slice(i * width, (i + 1) * width)
-        levels = (codes_ref[:, cols] - zero_ref[:, cols]).astype(jnp.float32).astype(jnp.bfloat16)
-        total += lax.dot_general(grads_ref[i], levels, (((1,), (1,)), ((), ())),
-                                 preferred_element_type=jnp.float32)
-    out_ref[...] = total
+    @pl.when(g >= groups)
+    def _():
+        width = held.shape[2]
+        total = out_ref[...]
+        for i in range(step):
+            cols = slice(i * width, (i + 1) * width)
+            levels = (codes_ref[:, cols] - zero_ref[:, cols]).astype(jnp.float32).astype(jnp.bfloat16)
+            total += lax.dot_general(held[(g - groups) * step + i], levels, (((1,), (1,)), ((), ())),
+                                     preferred_element_type=jnp.float32)
+        out_ref[...] = total
 
 
 def local(nr, nf, acts, out_grads, proj_in, proj_out, assignment, codes, zero_points, scales):
@@ -249,28 +296,25 @@
     rank = proj_in.shape[1]
     local_rank = rank // nf
     bf = jnp.bfloat16
-    parts = [jnp.dot(acts, proj_in, preferred_element_type=jnp.float32),
-             jnp.dot(out_grads, proj_out, preferred_element_type=jnp.float32)]
-
-    order = lax.iota(jnp.int32, tokens)
-    key = assignment * tokens + order
-    place = jnp.sum((key[:, None] < key[None, :]).astype(jnp.int32), axis=0)
-    hits = place[None, :] == order[:, None]
-    sorter = hits.astype(bf)
-    highs = [p.astype(bf) for p in parts]
-    lows = [(p - h.astype(jnp.float32)).astype(bf) for p, h in zip(parts, highs)]
-    both = jnp.dot(sorter, jnp.concatenate(highs + lows, 1), preferred_element_type=jnp.float32)
-    inner = (both[:, :rank] + both[:, 2 * rank:3 * rank]).reshape(nf, tokens // nf, rank)
-    ids = jnp.sum(jnp.where(hits, assignment[None, :], 0), axis=1).astype(jnp.float32)[:, None]
-    wide = -(-2 * local_rank // LANES) * LANES
-    high, low = both[:, rank:2 * rank].astype(bf), both[:, 3 * rank:].astype(bf)
-    fill = [jnp.zeros((tokens, wide - 2 * local_rank), bf)] if wide > 2 * local_rank else []
-    outer = jnp.stack([
-        jnp.concatenate([high[:, i * local_rank:(i + 1) * local_rank],
-                         low[:, i * local_rank:(i + 1) * local_rank]] + fill, 1) for i in range(nf)])
-
     vmem = pl.BlockSpec(memory_space=pltpu.VMEM)
     dma = pltpu.SemaphoreType.DMA
+    wide = -(-2 * local_rank // LANES) * LANES
+    block = tokens // 4
+    inner, outer, ids = pl.pallas_call(
+        functools.partial(project_kernel, nf),
+        out_shape=(jax.ShapeDtypeStruct((tokens, rank), jnp.float32),
+                   jax.ShapeDtypeStruct((nf, tokens, wide), bf),
+                   jax.ShapeDtypeStruct((tokens, 1), jnp.float32)),
+        grid=(4,),
+        in_specs=[vmem, vmem,
+                  pl.BlockSpec((block, acts.shape[1]), lambda i: (i, 0)),
+                  pl.BlockSpec((block, acts.shape[1]), lambda i: (i, 0)),
+                  vmem, vmem],
+        out_specs=(vmem, vmem, vmem),
+        scratch_shapes=[pltpu.VMEM((tokens, 4 * rank), bf)],
+        compiler_params=pltpu.CompilerParams(vmem_limit_bytes=40 * 2 ** 20),
+    )(assignment[None, :], assignment[:, None], acts, out_grads, proj_in, proj_out)
+    inner = inner.reshape(nf, tokens // nf, rank)
     in_all, out_all = pl.pallas_call(
         functools.partial(exchange_kernel, nr, nf, local_rank),
         out_shape=(jax.ShapeDtypeStruct((nr, tokens, rank), bf), jax.ShapeDtypeStruct((nr, tokens, wide), bf)),
@@ -296,34 +340,27 @@
     found = out_all[:, :, local_rank].astype(jnp.int32)
     starts = jnp.sum((found[:, None, :] < edges[None, :, None]).astype(jnp.int32), axis=2)
 
-    grads = pl.pallas_call(
-        grads_kernel,
-        out_shape=jax.ShapeDtypeStruct((local_rank, QUERIES, rank), bf),
-        grid=(QUERIES // GROUP,),
-        in_specs=[pl.BlockSpec(memory_space=pltpu.SMEM), vmem, vmem, vmem],
-        out_specs=pl.BlockSpec((local_rank, GROUP, rank), lambda g: (0, g, 0)),
+    stored, features = codes.shape
+    step = min(8, local_rank)
+    groups = QUERIES // GROUP
+    terms = pl.pallas_call(
+        functools.partial(score_kernel, step),
+        out_shape=jax.ShapeDtypeStruct((QUERIES, stored), jnp.float32),
+        grid=(groups + local_rank // step,),
+        in_specs=[
+            pl.BlockSpec(memory_space=pltpu.SMEM), vmem, vmem, vmem,
+            pl.BlockSpec((stored, step * rank), lambda i: (0, jnp.maximum(i - groups, 0))),
+            pl.BlockSpec((1, step * rank), lambda i: (0, jnp.maximum(i - groups, 0))),
+        ],
+        out_specs=vmem,
         scratch_shapes=[
             pltpu.VMEM((nr * WINDOW, rank), bf),
             pltpu.VMEM((nr * WINDOW, wide), jnp.float32),
             pltpu.VMEM((local_rank * GROUP, rank), jnp.float32),
+            pltpu.VMEM((local_rank, QUERIES, rank), bf),
         ],
         compiler_params=pltpu.CompilerParams(vmem_limit_bytes=56 * 2 ** 20),
-    )(starts, in_all, out_all, scales.reshape(local_rank, rank))
-
-    stored, features = codes.shape
-    step = min(8, local_rank)
-    terms = pl.pallas_call(
-        score_kernel,
-        out_shape=jax.ShapeDtypeStruct((QUERIES, stored), jnp.float32),
-        grid=(local_rank // step,),
-        in_specs=[
-            pl.BlockSpec((step, QUERIES, rank), lambda i: (i, 0, 0)),
-            pl.BlockSpec((stored, step * rank), lambda i: (0, i)),
-            pl.BlockSpec((1, step * rank), lambda i: (0, i)),
-        ],
-        out_specs=pl.BlockSpec((QUERIES, stored), lambda i: (0, 0)),
-        compiler_params=pltpu.CompilerParams(vmem_limit_bytes=56 * 2 ** 20),
-    )(grads, codes, zero_points.reshape(1, features))
+    )(starts, in_all, out_all, scales.reshape(local_rank, rank), codes, zero_points.reshape(1, features))
     return pl.pallas_call(
         functools.partial(total_kernel, nf),
         out_shape=jax.ShapeDtypeStruct((QUERIES // nf, stored), jnp.float32),

time: 123 us -> 112 us (0.911)
  matrix products: 7.32 us -> 0 us
  other arithmetic: 6.52 us -> 2.21 us
  Pallas kernels: 95.3 us -> 98.4 us
  local copies, waits for them, and re-layouts: 13.1 us -> 11.1 us
    dot_general x3 -> x0, matrix products: 7.32 us -> none  [the longest x1 3.63 us: local(): jnp.dot(acts, proj_in, preferred_element_type=jnp.float32)]
    unnamed x15, local copies, waits for them, and re-layouts: 3.54 us -> 8.89 us
    dot_general x1 -> x0, local copies, waits for them, and re-layouts: 3.34 us -> none  [local(): jnp.dot(sorter, jnp.concatenate(highs + lows, 1), preferred_element_type=...]
    pallas_call x2, Pallas kernels: 28.5 us -> 31.5 us  [the longest x1 25.3 us: local(): pl.pallas_call(functools.partial(score_kernel, step), out_shape=jax.Shape...]
    add x1 -> x0, local copies, waits for them, and re-layouts: 2.54 us -> none  [local(): both[:, :rank] + both[:, 2 * rank:3 * rank]]
    add x2 -> x0, other arithmetic: 1.93 us -> none  [the longest x1 1.15 us: local(): both[:, :rank] + both[:, 2 * rank:3 * rank]]
    reduce_sum x2 -> x0, other arithmetic: 1.66 us -> none  [the longest x1 1.19 us: local(): jnp.sum(jnp.where(hits, assignment[None, :], 0), axis=1).astype(jnp.float32)]
where the time goes in v3:
time: 112 us
  Pallas kernels  98.4 us (88%)
  local copies, waits for them, and re-layouts  11.1 us (10%)
  other arithmetic  2.21 us (2%)
    pallas_call x1, Pallas kernels, local(): pl.pallas_call(functools.partial(exchange_kernel, nr, nf, local_rank), ou...  61.2 us
    pallas_call x1, Pallas kernels, local(): pl.pallas_call(functools.partial(score_kernel, step), out_shape=jax.Shape...  25.3 us
    unnamed x15, local copies, waits for them, and re-layouts  8.89 us
    pallas_call x1, Pallas kernels, local(): pl.pallas_call(functools.partial(project_kernel, nf), out_shape=(jax.Shap...  6.17 us
    pallas_call x1, Pallas kernels, local(): pl.pallas_call(functools.partial(total_kernel, nf), out_shape=jax.ShapeDt...  5.69 us

profile of v3, /device:TPU:0, one launch (start us, length us, event | category | flops | bytes accessed | tf_op | source)
XLA Modules:
  0.0 111.8 jit_solution(6924073329252821077)
XLA Ops:
  0.0 0.9 copy.10.col_ref
  0.9 0.0 copy-start.1
  0.9 2.2 %copy-done.1 = bf16[1024,2048]{1,0:T(8,128)(2,1)S(1)} copy-done((bf16[1024,2048]{1,0:T(8,128)(2,1)S(1)}, bf16[1024,2048]{1,0:T(8,128)(2,1)}, u32[]{:S(2)}) %copy-start.1) | copy-done | bytes 4194328
  3.1 0.0 copy-start.2
  3.1 2.2 %copy-done.2 = bf16[1024,2048]{1,0:T(8,128)(2,1)S(1)} copy-done((bf16[1024,2048]{1,0:T(8,128)(2,1)S(1)}, bf16[1024,2048]{1,0:T(8,128)(2,1)}, u32[]{:S(2)}) %copy-start.2) | copy-done | bytes 4194328
  5.3 0.0 copy-start.3
  5.3 1.2 %copy-done.3 = bf16[2048,256]{1,0:T(8,128)(2,1)S(1)} copy-done((bf16[2048,256]{1,0:T(8,128)(2,1)S(1)}, bf16[2048,256]{1,0:T(8,128)(2,1)}, u32[]{:S(2)}) %copy-start.3) | copy-done | bytes 1048600
  6.5 0.0 copy-start.4
  6.5 1.2 %copy-done.4 = bf16[2048,256]{1,0:T(8,128)(2,1)S(1)} copy-done((bf16[2048,256]{1,0:T(8,128)(2,1)S(1)}, bf16[2048,256]{1,0:T(8,128)(2,1)}, u32[]{:S(2)}) %copy-start.4) | copy-done | bytes 1048600
  7.7 0.0 copy-start.5
  7.7 0.7 copy-done.5
  8.4 6.2 %shard_map.82 = (f32[1024,256]{1,0:T(8,128)S(1)}, bf16[4,1024,128]{2,1,0:T(8,128)(2,1)S(1)}, f32[1024,1]{1,0:T(8,128)S(1)}) custom-call(s32[1,1024]{1,0:T(1,128)S(1)} %bitcast.6, s32[1024,1]{1,0:T(8,128)S(1)} %copy.10.col_ref, bf16[1024,2048]{1,0:T(8,128)(2,1)S(1)} %copy-done.1, bf16[1024,2048]{1,0:T(8,128)(2,1)S(1)} %copy-done.2, ...), custom_call_target="tpu_custom_call" | custom-call | tf_op jit(solution)/shard_map/pallas_call | solution.py:303
  14.6 0.0 copy-start.6
  14.6 61.2 %shard_map.83 = (bf16[8,1024,256]{2,1,0:T(8,128)(2,1)}, bf16[8,1024,128]{2,1,0:T(8,128)(2,1)S(1)}) custom-call(f32[4,256,256]{2,1,0:T(8,128)S(1)} %bitcast.4, bf16[4,1024,128]{2,1,0:T(8,128)(2,1)S(1)} %get-tuple-element.11.outer_ref, f32[1024,1]{1,0:T(8,128)S(1)} %get-tuple-element.12.ids_ref), custom_call_target="tpu_custom_call" | custom-call | tf_op jit(solution)/shard_map/pallas_call | solution.py:318
  75.8 0.0 copy-start
  75.9 1.7 %convert_reduce_fusion = s32[8,1024]{1,0:T(8,128)S(1)} fusion(bf16[8,1024,128]{2,1,0:T(8,128)(2,1)S(1)} %get-tuple-element.13.outer_ref), kind=kLoop, calls=%fused_computation | loop fusion | flops 8192 | bytes 49152 | tf_op jit(solution)/shard_map/convert_element_type | solution.py:340
  77.6 0.5 convert_reduce_fusion.1
  78.1 0.7 copy.11.starts_ref
  78.8 0.0 copy-done.6
  78.8 0.6 reshape.21.scales_ref
  79.4 0.0 copy-done
  79.4 25.3 %shard_map.84.terms_ref = f32[256,128]{1,0:T(8,128)} custom-call(s32[8,17]{1,0:T(8,128)} %copy.11.starts_ref, bf16[8,1024,256]{2,1,0:T(8,128)(2,1)} %get-tuple-element.14.inner_ref, bf16[8,1024,128]{2,1,0:T(8,128)(2,1)} %copy-done, f32[64,256]{1,0:T(8,128)} %reshape.21.scales_ref, s32[128,16384]{1,0:T(8,128)} %codes_ref.1, s32[1,16384]{1,0:T(1,128)} %bitcast.7), custom_call_target="tpu_custom_call" | custom-call | tf_op jit(solution)/shard_map/pallas_call | solution.py:346
  104.7 5.7 %shard_map.85 = f32[64,128]{1,0:T(8,128)} custom-call(f32[256,128]{1,0:T(8,128)} %shard_map.84.terms_ref), custom_call_target="tpu_custom_call" | custom-call | tf_op jit(solution)/shard_map/pallas_call | solution.py:364
  110.4 1.4 %copy.13 = f32[64,128]{1,0:T(8,128)} copy(f32[64,128]{1,0:T(8,128)} %shard_map.85) | data formatting | bytes 65536
  (1 shorter events, 0.0 us)
Async XLA Ops:
  0.9 2.2 %copy-start.1 = (bf16[1024,2048]{1,0:T(8,128)(2,1)S(1)}, bf16[1024,2048]{1,0:T(8,128)(2,1)}, u32[]{:S(2)}) copy-start(bf16[1024,2048]{1,0:T(8,128)(2,1)} %acts_ref.1) | copy-start | bytes 12582916
  3.1 2.2 %copy-start.2 = (bf16[1024,2048]{1,0:T(8,128)(2,1)S(1)}, bf16[1024,2048]{1,0:T(8,128)(2,1)}, u32[]{:S(2)}) copy-start(bf16[1024,2048]{1,0:T(8,128)(2,1)} %grads_ref.1) | copy-start | bytes 12582916
  5.3 1.2 %copy-start.3 = (bf16[2048,256]{1,0:T(8,128)(2,1)S(1)}, bf16[2048,256]{1,0:T(8,128)(2,1)}, u32[]{:S(2)}) copy-start(bf16[2048,256]{1,0:T(8,128)(2,1)} %in_ref.1) | copy-start | bytes 3145732
  6.5 1.2 %copy-start.4 = (bf16[2048,256]{1,0:T(8,128)(2,1)S(1)}, bf16[2048,256]{1,0:T(8,128)(2,1)}, u32[]{:S(2)}) copy-start(bf16[2048,256]{1,0:T(8,128)(2,1)} %out_ref.1) | copy-start | bytes 3145732
  7.7 0.7 copy-start.5
  14.6 64.1 %copy-start.6 = (f32[16384]{0:T(1024)S(1)}, f32[16384]{0:T(1024)}, u32[]{:S(2)}) copy-start(f32[16384]{0:T(1024)} %param.15) | copy-start | bytes 196612
  75.8 3.5 %copy-start = (bf16[8,1024,128]{2,1,0:T(8,128)(2,1)}, bf16[8,1024,128]{2,1,0:T(8,128)(2,1)S(1)}, u32[]{:S(2)}) copy-start(bf16[8,1024,128]{2,1,0:T(8,128)(2,1)S(1)} %get-tuple-element.13.outer_ref) | copy-start | bytes 6291460

commit v4 on v3

--- a/solution.py
+++ b/solution.py
@@ -101,35 +101,29 @@
         return jnp.where(lane < local_rank, high, low).astype(jnp.bfloat16)
 
     near = {}
-    for d in list(range(1, half)) + [0]:
-        to = lax.rem(core + 2 * d, nf)
-        near[d] = (begin(inner_ref.at[to], rin.at[d], rs_send.at[0, d], rs_recv.at[0, d], (row, core)),
-                   begin(outer_ref.at[to], rout.at[d], rs_send.at[1, d], rs_recv.at[1, d], (row, core)))
+    turns = list(range(1, half)) + [0]
+    for w, src, dst in ((0, inner_ref, rin), (1, outer_ref, rout)):
+        for d in turns:
+            to = lax.rem(core + 2 * d, nf)
+            near[d, w] = begin(src.at[to], dst.at[d], rs_send.at[w, d], rs_recv.at[w, d], (row, core))
     far = {}
     for d in range(1, half):
         to = lax.rem(me + 2 * d, nf)
-        near[d][0].wait_recv()
+        near[d, 0].wait_recv()
         to_in[d - 1] = inner_ref[to] + rin[d]
-        one = begin(to_in.at[d - 1], far_in.at[d - 1], far_send.at[0, d], far_recv.at[0, d], (row, to))
-        near[d][1].wait_recv()
+        far[d, 0] = begin(to_in.at[d - 1], far_in.at[d - 1], far_send.at[0, d], far_recv.at[0, d], (row, to))
+    for d in range(1, half):
+        to = lax.rem(me + 2 * d, nf)
+        near[d, 1].wait_recv()
         to_out[d - 1] = pack(unpack(outer_ref[to]) + unpack(rout[d]))
-        two = begin(to_out.at[d - 1], far_out.at[d - 1], far_send.at[1, d], far_recv.at[1, d], (row, to))
-        far[d] = (one, two)
+        far[d, 1] = begin(to_out.at[d - 1], far_out.at[d - 1], far_send.at[1, d], far_recv.at[1, d], (row, to))
     mine = pl.ds(pl.multiple_of(me * tq, tq), tq)
-    near[0][0].wait_recv()
+    near[0, 0].wait_recv()
     total = inner_ref[me] + rin[0]
     for d in range(1, half):
-        far[d][0].wait_recv()
+        far[d, 0].wait_recv()
         total += far_in[d - 1]
     in_all[row, mine, :] = total.astype(jnp.bfloat16)
-    near[0][1].wait_recv()
-    total = unpack(outer_ref[me]) + unpack(rout[0])
-    for d in range(1, half):
-        far[d][1].wait_recv()
-        total += unpack(far_out[d - 1])
-    total = jnp.where(lane < local_rank, total, jnp.where(lane == local_rank, ids_ref[...], 0.0))
-    out_all[row] = total.astype(jnp.bfloat16)
-
     steps_r = nr // 2
     steps_l = nr - 1 - steps_r
 
@@ -177,25 +171,40 @@
             sends.append(c)
             tails.append(c)
 
-    cr = launch(0, right, 0)
-    cl = launch(0, left, steps_r)
+    cr = launch(0, right, 0, (0,))
+    cl = launch(0, left, steps_r, (0,))
     spread(0)
+    near[0, 1].wait_recv()
+    total = unpack(outer_ref[me]) + unpack(rout[0])
+    for d in range(1, half):
+        far[d, 1].wait_recv()
+        total += unpack(far_out[d - 1])
+    total = jnp.where(lane < local_rank, total, jnp.where(lane == local_rank, ids_ref[...], 0.0))
+    out_all[row] = total.astype(jnp.bfloat16)
+    dr = launch(0, right, 0, (1,))
+    dl = launch(0, left, steps_r, (1,))
     late = [0]
     for s in range(steps_r):
-        e = 1 + s
+        e, el = 1 + s, 1 + steps_r + s
         fresh = [e]
         for c in cr:
             c.wait_recv()
         if s + 1 < steps_r:
-            cr = launch(e, right, s + 1, (0, 1) if s + 2 < steps_r else (0,))
+            cr = launch(e, right, s + 1, (0,))
         spread(e)
-        for c in cl:
+        if s < steps_l:
+            for c in cl:
+                c.wait_recv()
+            cl = launch(el, left, el, (0,)) if s + 1 < steps_l else []
+            spread(el)
+            fresh.append(el)
+        for c in dr:
+            c.wait_recv()
+        dr = launch(e, right, s + 1, (1,)) if s + 2 < steps_r else []
+        for c in dl:
             c.wait_recv()
         if s < steps_l:
-            e = 1 + steps_r + s
-            cl = launch(e, left, steps_r + s + 1, (0, 1) if s + 1 < steps_l else (1,))
-            spread(e)
-            fresh.append(e)
+            dl = launch(el, left, el, (1,))
         for e in late:
             pass_on(e)
         late = fresh
@@ -312,7 +321,7 @@
                   vmem, vmem],
         out_specs=(vmem, vmem, vmem),
         scratch_shapes=[pltpu.VMEM((tokens, 4 * rank), bf)],
-        compiler_params=pltpu.CompilerParams(vmem_limit_bytes=40 * 2 ** 20),
+        compiler_params=pltpu.CompilerParams(vmem_limit_bytes=56 * 2 ** 20),
     )(assignment[None, :], assignment[:, None], acts, out_grads, proj_in, proj_out)
     inner = inner.reshape(nf, tokens // nf, rank)
     in_all, out_all = pl.pallas_call(

time: 112 us -> 108 us (0.964)
  local copies, waits for them, and re-layouts: 11.1 us -> 7.89 us
    pallas_call x1, Pallas kernels: 61.2 us -> 55.5 us  [local(): pl.pallas_call(functools.partial(exchange_kernel, nr, nf, local_rank), ou...]
    pallas_call x1, Pallas kernels: 6.17 us -> 11.1 us  [local(): pl.pallas_call(functools.partial(project_kernel, nf), out_shape=(jax.Shap...]
    unnamed x15 -> x11, local copies, waits for them, and re-layouts: 8.89 us -> 4.87 us
where the time goes in v4:
time: 108 us
  Pallas kernels  97.5 us (90%)
  local copies, waits for them, and re-layouts  7.89 us (7%)
  other arithmetic  2.21 us (2%)
    pallas_call x1, Pallas kernels, local(): pl.pallas_call(functools.partial(exchange_kernel, nr, nf, local_rank), ou...  55.5 us
    pallas_call x1, Pallas kernels, local(): pl.pallas_call(functools.partial(score_kernel, step), out_shape=jax.Shape...  25.3 us
    pallas_call x1, Pallas kernels, local(): pl.pallas_call(functools.partial(project_kernel, nf), out_shape=(jax.Shap...  11.1 us
    pallas_call x1, Pallas kernels, local(): pl.pallas_call(functools.partial(total_kernel, nf), out_shape=jax.ShapeDt...  5.69 us
    unnamed x11, local copies, waits for them, and re-layouts  4.87 us

profile of v4, /device:TPU:0, one launch (start us, length us, event | category | flops | bytes accessed | tf_op | source)
XLA Modules:
  0.0 107.7 jit_solution(9828512208781142394)
XLA Ops:
  0.0 1.7 %copy.10.col_ref = s32[1024,1]{1,0:T(8,128)} copy(s32[1024,1]{0,1:T(1,128)} %bitcast.6) | data formatting | bytes 8192 | tf_op jit(solution)/shard_map/broadcast_in_dim | solution.py:325
  1.7 0.0 copy-start.4
  1.7 11.1 %shard_map.82 = (f32[1024,256]{1,0:T(8,128)}, bf16[4,1024,128]{2,1,0:T(8,128)(2,1)}, f32[1024,1]{1,0:T(8,128)}) custom-call(s32[1,1024]{1,0:T(1,128)} %bitcast.7, s32[1024,1]{1,0:T(8,128)} %copy.10.col_ref, bf16[1024,2048]{1,0:T(8,128)(2,1)} %acts_ref.1, bf16[1024,2048]{1,0:T(8,128)(2,1)} %grads_ref.1, bf16[2048,256]{1,0:T(8,128)(2,1)} %in_ref.1, ...), custom_call_target="tpu_custom_call" | custom-call | tf_op jit(solution)/shard_map/pallas_call | solution.py:312
  12.8 0.0 copy-start.1
  12.8 1.2 %copy-done.1 = f32[1024,256]{1,0:T(8,128)S(1)} copy-done((f32[1024,256]{1,0:T(8,128)S(1)}, f32[1024,256]{1,0:T(8,128)}, u32[]{:S(2)}) %copy-start.1) | copy-done | bytes 1048600
  14.0 0.0 copy-start.2
  14.0 1.2 %copy-done.2 = bf16[4,1024,128]{2,1,0:T(8,128)(2,1)S(1)} copy-done((bf16[4,1024,128]{2,1,0:T(8,128)(2,1)S(1)}, bf16[4,1024,128]{2,1,0:T(8,128)(2,1)}, u32[]{:S(2)}) %copy-start.2) | copy-done | bytes 1048600
  15.2 0.0 copy-start.3
  15.2 1.0 copy-done.3
  16.3 55.5 %shard_map.83 = (bf16[8,1024,256]{2,1,0:T(8,128)(2,1)}, bf16[8,1024,128]{2,1,0:T(8,128)(2,1)S(1)}) custom-call(f32[4,256,256]{2,1,0:T(8,128)S(1)} %bitcast.4, bf16[4,1024,128]{2,1,0:T(8,128)(2,1)S(1)} %copy-done.2, f32[1024,1]{1,0:T(8,128)S(1)} %copy-done.3), custom_call_target="tpu_custom_call" | custom-call | tf_op jit(solution)/shard_map/pallas_call | solution.py:327
  71.7 0.0 copy-start
  71.8 1.7 %convert_reduce_fusion = s32[8,1024]{1,0:T(8,128)S(1)} fusion(bf16[8,1024,128]{2,1,0:T(8,128)(2,1)S(1)} %get-tuple-element.13.outer_ref), kind=kLoop, calls=%fused_computation | loop fusion | flops 8192 | bytes 49152 | tf_op jit(solution)/shard_map/convert_element_type | solution.py:349
  73.5 0.5 convert_reduce_fusion.1
  74.0 0.7 copy.11.starts_ref
  74.6 0.0 copy-done.4
  74.7 0.6 reshape.21.scales_ref
  75.3 0.0 copy-done
  75.3 25.3 %shard_map.84.terms_ref = f32[256,128]{1,0:T(8,128)} custom-call(s32[8,17]{1,0:T(8,128)} %copy.11.starts_ref, bf16[8,1024,256]{2,1,0:T(8,128)(2,1)} %get-tuple-element.14.inner_ref, bf16[8,1024,128]{2,1,0:T(8,128)(2,1)} %copy-done, f32[64,256]{1,0:T(8,128)} %reshape.21.scales_ref, s32[128,16384]{1,0:T(8,128)} %codes_ref.1, s32[1,16384]{1,0:T(1,128)} %bitcast.5), custom_call_target="tpu_custom_call" | custom-call | tf_op jit(solution)/shard_map/pallas_call | solution.py:355
  100.6 5.7 %shard_map.85 = f32[64,128]{1,0:T(8,128)} custom-call(f32[256,128]{1,0:T(8,128)} %shard_map.84.terms_ref), custom_call_target="tpu_custom_call" | custom-call | tf_op jit(solution)/shard_map/pallas_call | solution.py:373
  106.3 1.4 %copy.13 = f32[64,128]{1,0:T(8,128)} copy(f32[64,128]{1,0:T(8,128)} %shard_map.85) | data formatting | bytes 65536
  (1 shorter events, 0.0 us)
Async XLA Ops:
  1.7 72.9 %copy-start.4 = (f32[16384]{0:T(1024)S(1)}, f32[16384]{0:T(1024)}, u32[]{:S(2)}) copy-start(f32[16384]{0:T(1024)} %param.15) | copy-start | bytes 196612
  12.8 1.2 %copy-start.1 = (f32[1024,256]{1,0:T(8,128)S(1)}, f32[1024,256]{1,0:T(8,128)}, u32[]{:S(2)}) copy-start(f32[1024,256]{1,0:T(8,128)} %get-tuple-element.10) | copy-start | bytes 3145732
  14.0 1.2 %copy-start.2 = (bf16[4,1024,128]{2,1,0:T(8,128)(2,1)S(1)}, bf16[4,1024,128]{2,1,0:T(8,128)(2,1)}, u32[]{:S(2)}) copy-start(bf16[4,1024,128]{2,1,0:T(8,128)(2,1)} %get-tuple-element.11.outer_ref) | copy-start | bytes 3145732
  15.2 1.0 copy-start.3
  71.7 3.5 %copy-start = (bf16[8,1024,128]{2,1,0:T(8,128)(2,1)}, bf16[8,1024,128]{2,1,0:T(8,128)(2,1)S(1)}, u32[]{:S(2)}) copy-start(bf16[8,1024,128]{2,1,0:T(8,128)(2,1)S(1)} %get-tuple-element.13.outer_ref) | copy-start | bytes 6291460
